TPU v7x, 128 devices: a whole 4x4x4 slice. The times are simulated.
128 devices in a mesh: island: 4 (over y_lo, core), mp: 32 (over z, x, y_hi).
Axes of the slice: x: 4, y: 4 (y_hi: 2, y_lo: 2; y = y_hi * 2 + y_lo), z: 4, core: 2. Of those that a mesh axis runs over, the one named last changes fastest.
Arguments:
- hidden: bfloat16 [4, 4096, 14336], P('island', None, 'mp'), may hold values from -6 to 6
- cotangent: bfloat16 [4, 4096, 4096], P('island', 'mp'), may hold values from -6 to 6
- local_weight: bfloat16 [4, 4096, 14336], P('island', None, 'mp'), may hold values from -6 to 6
- pending: bfloat16 [4, 4096, 14336], P('island', None, 'mp'), may hold values from -3 to 3
- global_weight: float32 [4096, 14336], P('island', 'mp'), may hold values from -6 to 6
- outer_momentum: float32 [4096, 14336], P('island', 'mp'), may hold values from -3 to 3
Outputs:
- hidden_grad: bfloat16 [4, 4096, 14336], P('island', None, 'mp')
- merged_weight: bfloat16 [4, 4096, 14336], P('island', None, 'mp')
- new_global: float32 [4096, 14336], P('island', 'mp')
- new_momentum: float32 [4096, 14336], P('island', 'mp')
All inputs are finite; a program needn't handle non-finite values.
Results may differ from a plain program's by a relative error of at most 0.0065.
Values may be sent and summed in bfloat16 or wider, within the bound.
A program may use at most 128 MiB of HBM per device.

v0:
```python
import math

import jax
import jax.numpy as jnp
from jax import lax
from jax.sharding import PartitionSpec as P

D = 4096


inner_rate = 0.3
outer_rate = 0.7
decay_rate = 0.9
mix_weight = 0.5


def body(hidden, cotangent, local_weight, pending, global_weight, outer_momentum):
    activation = hidden[0]
    grads_out = cotangent[0]
    weight = local_weight[0]
    tokens = activation.shape[0]
    columns = weight.shape[0]
    backward_scale = 1.0 / math.sqrt(D)
    grad_scale = 1.0 / math.sqrt(tokens)
    islands = lax.axis_size("island")
    contract_tokens = (((0,), (0,)), ((), ()))
    piece = lax.all_gather(grads_out, "mp", axis=0, tiled=True)
    total = lax.dot_general(piece, activation, contract_tokens, preferred_element_type=jnp.float32)
    block = jnp.dot(piece, weight, preferred_element_type=jnp.float32) * backward_scale
    grad_hidden = block.astype(jnp.bfloat16)
    total, grad_hidden = (total, grad_hidden)
    weight_grad = total * grad_scale
    share = columns // islands
    summed_all = lax.psum(pending[0], "island").astype(jnp.float32)
    mean_share = (
        lax.dynamic_slice_in_dim(summed_all, lax.axis_index("island") * share, share, 0) / islands
    )
    new_momentum = decay_rate * outer_momentum + mean_share
    new_global = global_weight - outer_rate * (mean_share + decay_rate * new_momentum)
    fresh = lax.all_gather(new_global.astype(jnp.bfloat16), "island", axis=0, tiled=True)
    merged = mix_weight * (weight.astype(jnp.float32) - inner_rate * weight_grad) + (
        1.0 - mix_weight
    ) * fresh.astype(jnp.float32)
    return (grad_hidden[None], merged.astype(jnp.bfloat16)[None], new_global, new_momentum)


def solution(mesh):
    placed = (
        P("island", None, "mp"),
        P("island", "mp", None),
        P("island", None, "mp"),
        P("island", None, "mp"),
        P("island", "mp"),
        P("island", "mp"),
    )
    return jax.shard_map(
        body,
        mesh=mesh,
        in_specs=placed,
        out_specs=(
            P("island", None, "mp"),
            P("island", None, "mp"),
            P("island", "mp"),
            P("island", "mp"),
        ),
        check_vma=False,
    )
```

profile of v0, /device:TPU:1, one launch (start us, length us, event | category | flops | bytes accessed | tf_op | source)
XLA Modules:
  0.0 358.5 jit_solution(4233023786497599555)
XLA Ops:
  8.0 0.0 copy-start
  8.0 0.0 all-reduce.2.cloned.1.call-start
  8.1 0.7 all-reduce.2.cloned.1.call-update
  8.7 0.0 all-gather.6.cloned.1.call-start
  8.8 0.5 all-gather.6.cloned.1.call-update
  9.3 0.0 all-gather.4.cloned.1.call-start
  9.4 115.1 %all-reduce.2.cloned.1.call-done = bf16[4096,448]{0,1:T(8,128)(2,1)} async-done(((bf16[4096,448]{0,1:T(8,128)(2,1)}), bf16[4096,448]{0,1:T(8,128)(2,1)}) %all-reduce.2.cloned.1.call-update) | async-done | bytes 3670032 | tf_op jit(solution)/shard_map/psum | solution.py:34
  124.5 0.0 copy-done
  124.5 5.8 %fusion.16 = (bf16[1024,448]{0,1:T(8,128)(2,1)}, f32[1024,448]{0,1:T(8,128)}, f32[1024,448]{0,1:T(8,128)}) fusion(f32[1024,448]{0,1:T(8,128)S(1)} %copy-done, bf16[4096,448]{0,1:T(8,128)(2,1)} %all-reduce.2.cloned.1.call-done, s32[]{:T(128)S(6)} %select_n.3, f32[1024,448]{0,1:T(8,128)} %param.11), kind=kLoop, calls=%fused_computation.13 | loop fusion | flops 4128768 | bytes 9175044 | tf_op jit(solution)/shard_map/convert_element_type | solution.py:40
  130.2 0.0 all-gather.4.cloned.1.call-update
  130.3 152.0 %all-gather.6.cloned.1.call-done = bf16[1,4096,4096]{2,1,0:T(8,128)(2,1)} async-done(((bf16[1,128,4096]{2,1,0:T(8,128)(2,1)}), bf16[1,4096,4096]{2,1,0:T(8,128)(2,1)}) %all-gather.6.cloned.1.call-update) | async-done | bytes 33554448 | tf_op jit(solution)/shard_map/all_gather | solution.py:27
  282.3 23.6 %fusion.8 = bf16[1,4096,448]{1,2,0:T(8,128)(2,1)} fusion(bf16[1,4096,4096]{2,1,0:T(8,128)(2,1)} %all-gather.6.cloned.1.call-done, bf16[1,4096,448]{1,2,0:T(8,128)(2,1)} %param.8), kind=kOutput, calls=%fused_computation.6 | convolution fusion | flops 15036055552 | bytes 40894464 | tf_op jit(solution)/shard_map/dot_general | solution.py:29
  305.9 19.3 %all-gather.4.cloned.1.call-done = bf16[4096,448]{0,1:T(8,128)(2,1)} async-done(((bf16[1024,448]{0,1:T(8,128)(2,1)}), bf16[4096,448]{0,1:T(8,128)(2,1)}) %all-gather.4.cloned.1.call-update) | async-done | bytes 3670032 | tf_op jit(solution)/shard_map/all_gather | solution.py:40
  325.1 25.9 %fusion.11 = bf16[1,4096,448]{1,2,0:T(8,128)(2,1)} fusion(bf16[4096,448]{0,1:T(8,128)(2,1)} %all-gather.4.cloned.1.call-done, bf16[1,4096,4096]{2,1,0:T(8,128)(2,1)} %all-gather.6.cloned.1.call-done, bf16[1,4096,448]{1,2,0:T(8,128)(2,1)} %param.6, bf16[1,4096,448]{1,2,0:T(8,128)(2,1)} %param.8), kind=kOutput, calls=%fused_computation.7 | convolution fusion | flops 15045230592 | bytes 48234496 | tf_op jit(solution)/shard_map/dot_general | solution.py:28
Async XLA Ops:
  8.0 116.5 %copy-start = (f32[1024,448]{0,1:T(8,128)S(1)}, f32[1024,448]{0,1:T(8,128)}, u32[]{:S(2)}) copy-start(f32[1024,448]{0,1:T(8,128)} %param.10) | copy-start | bytes 5505028
  8.0 116.5 %all-reduce.2.cloned.1.call-start = ((), (), s32[]{:S(2)}) async-start(), calls=%async_computation | async-start | bytes 7340032 | tf_op jit(solution)/shard_map/psum | solution.py:34
  8.7 273.6 %all-gather.6.cloned.1.call-start = ((), (), s32[]{:S(2)}) async-start(), calls=%async_computation.2 | async-start | bytes 34603008 | tf_op jit(solution)/shard_map/all_gather | solution.py:27
  9.3 315.8 %all-gather.4.cloned.1.call-start = ((), (), s32[]{:S(2)}) async-start(), calls=%async_computation.1 | async-start | bytes 4587520 | tf_op jit(solution)/shard_map/all_gather | solution.py:40
Sparse Core Ops, SparseCore 0:
  11.4 113.0 all-reduce.1
Sparse Core Ops, SparseCore 1:
  12.2 270.0 all-gather.5
  284.4 40.7 all-gather.3
where the time goes:
time: 359 us
  waiting for transfers between devices  288 us (80%)
  matrix products  49.5 us (14%)
  between operations  15.5 us (4%)
  other arithmetic  5.76 us (2%)
    all_gather x1, waiting for transfers between devices, body(): piece = lax.all_gather(grads_out, 'mp', axis=0, tiled=True)  152 us
    psum x1, waiting for transfers between devices, body(): summed_all = lax.psum(pending[0], 'island').astype(jnp.float32)  115 us
    dot_general x1, matrix products, body(): lax.dot_general(piece, activation, contract_tokens, preferred_element_typ...  25.9 us
    dot_general x1, matrix products, body(): jnp.dot(piece, weight, preferred_element_type=jnp.float32) * backward_scale  23.6 us
    all_gather x1, waiting for transfers between devices, body(): lax.all_gather(new_global.astype(jnp.bfloat16), 'island', axis=0, tiled=T...  19.3 us
  transfers between devices with their start and end apart: 3, of which 3 were waited for; matrix products, arithmetic and copies ran while one was open for 8% of the time, Pallas kernels for 0%

commit v1 on v0

v1 whole, which is shorter than its diff:
```python
import math

import jax
import jax.numpy as jnp
from jax import lax
from jax.experimental import pallas as pl
from jax.experimental.pallas import tpu as pltpu
from jax.sharding import PartitionSpec as P

D = 4096
TOKENS = 4096
FF_SHARE = 448
SHARD = 128

inner_rate = 0.3
outer_rate = 0.7
decay_rate = 0.9
mix_weight = 0.5
islands = 4

MESH = pl.DeviceIdType.MESH
MIB = 2**20

PIECES = (
    (0, 32, 0, True, 1),
    (32, 16, 0, True, -1),
    (48, 16, 0, False, -1),
    (64, 32, 1, True, 1),
    (96, 16, 1, True, -1),
    (112, 16, 1, False, -1),
)
LINKS = ((0, 1), (0, -1), (1, 1), (1, -1), (2, 1))
WRAP = (4, 4, 2)


def moved(offset, link):
    axis, step = LINKS[link]
    out = list(offset)
    out[axis] = (out[axis] + step) % WRAP[axis]
    return tuple(out)


def links_of(piece, offset):
    _, _, first, early, way = PIECES[piece]
    second = 1 - first
    found = []
    if offset[2] == 0 and (offset[first], offset[second]) == (0, 0) and early:
        found.append(4)
    if early or offset[2] == 0:
        for axis in (first, second):
            if axis == first and offset[second] != 0:
                continue
            turn = way if axis == first or offset[first] % 2 == 0 else -way
            for step in (1, -1):
                link = LINKS.index((axis, step))
                if offset[axis] == 0 or (offset[axis] == step % 4 and turn == step):
                    found.append(link)
    if offset[2] == 0 and not early:
        found.append(4)
    return found


def depth_of(piece, offset):
    best = 0.0
    for link in links_of(piece, offset):
        best = max(best, 1.0 + depth_of(piece, moved(offset, link)))
    return best


def plan():
    unit = 2.87 / 16
    latency = 2.0
    hg_time, wg_time = 2.2, 2.2
    heaps = [[] for _ in LINKS]
    free_at = [0.0] * len(LINKS)
    queued = [[] for _ in LINKS]
    arrivals = []
    steps = []
    have = {}
    now = 0.0
    sent_rows = [0] * len(LINKS)
    todo_hg, todo_wg = [], []
    islands_due = [(8.0, "reduce"), (34.0, "outer"), (62.0, "relay"), (76.0, "blend")]
    pieces = range(len(PIECES))

    def offer(item):
        for link in links_of(*item):
            heaps[link].append((-depth_of(item[0], moved(item[1], link)), now, item))

    def pump():
        for link in range(len(LINKS)):
            while True:
                queued[link] = [t for t in queued[link] if t > now]
                if len(queued[link]) >= 3 or not heaps[link]:
                    break
                heaps[link].sort()
                _, _, item = heaps[link].pop(0)
                rows = PIECES[item[0]][1]
                start = max(now, free_at[link])
                free_at[link] = start + unit * rows
                queued[link].append(free_at[link])
                sent_rows[link] += rows
                steps.append(("send", item, link))
                arrivals.append((free_at[link] + latency, (item[0], moved(item[1], link))))

    def land(item):
        have[item] = True
        offset = item[1]
        pair = offset[:2]
        if all((p, pair + (dy,)) in have for p in pieces for dy in (0, 1)):
            todo_hg.append(pair)
            todo_wg.append(pair)

    for p in pieces:
        item = (p, (0, 0, 0))
        have[item] = True
        offer(item)
    pump()
    total = len(PIECES) * 32
    first_wg = True
    while len(have) < total or todo_hg or todo_wg or islands_due:
        arrivals.sort()
        while arrivals and arrivals[0][0] <= now:
            _, item = arrivals.pop(0)
            steps.append(("wait", item))
            land(item)
            offer(item)
            now += 0.06
        pump()
        if islands_due and islands_due[0][0] <= now and not (islands_due[0][1] == "blend" and first_wg):
            steps.append(("task", islands_due.pop(0)[1]))
            now += 4.0
        elif todo_hg and len(todo_hg) >= len(todo_wg):
            steps.append(("task", "hg", todo_hg.pop(0)))
            now += hg_time
        elif todo_wg:
            steps.append(("task", "wg", todo_wg.pop(0), first_wg))
            first_wg = False
            now += wg_time
        else:
            times = [t for t, _ in arrivals[:1]] + [t for t, _ in islands_due[:1]]
            for q in queued:
                if len(q) >= 3:
                    times.append(min(q))
            times = [t for t in times if t > now]
            now = min(times) if times else now + 0.1
    last = max(i for i, s in enumerate(steps) if s[0] == "task" and s[1] == "wg")
    steps[last] = ("task", "end") + steps[last][2:3]
    return steps, sent_rows, now


def kernel(
    hidden, cotangent, local_weight, pending, global_weight, outer_momentum,
    hidden_grad, merged, new_global, new_momentum, fresh,
    c_buf, h_buf, w_buf, acc, hg_buf, p_buf, pc_buf, py_buf, g_buf, m_buf,
    send_sem, recv_sem, load_sem, hg_sem, out_sem, isl_send, isl_recv,
):
    island = lax.axis_index("island")
    mp = lax.axis_index("mp")
    z, x, yh = mp // 8, (mp // 2) % 4, mp % 2
    core, yl = island % 2, island // 2

    def mp_at(pz, px, py):
        return (lax.rem(pz, 4) * 4 + lax.rem(px, 4)) * 2 + lax.rem(py, 2)

    partner = [
        {"mp": mp_at(z + 1, x, yh)},
        {"mp": mp_at(z + 3, x, yh)},
        {"mp": mp_at(z, x + 1, yh)},
        {"mp": mp_at(z, x + 3, yh)},
        {"mp": mp_at(z, x, yh + 1)},
    ]
    other_core = {"island": yl * 2 + 1 - core}
    other_y = {"island": (1 - yl) * 2 + core}

    loads = [
        pltpu.make_async_copy(cotangent.at[0], c_buf.at[pl.ds(pl.multiple_of(mp * SHARD, SHARD), SHARD)], load_sem.at[0]),
        pltpu.make_async_copy(local_weight.at[0], w_buf, load_sem.at[1]),
        pltpu.make_async_copy(hidden.at[0], h_buf, load_sem.at[2]),
        pltpu.make_async_copy(global_weight, g_buf, load_sem.at[3]),
        pltpu.make_async_copy(outer_momentum, m_buf, load_sem.at[4]),
    ]

    def quarter(ref, index):
        return ref.at[pl.ds(pl.multiple_of(index * 1024, 1024), 1024)]

    mine, theirs = yl * 2 + core, (1 - yl) * 2 + core
    p_loads = [
        pltpu.make_async_copy(quarter(pending.at[0], theirs), p_buf.at[0], load_sem.at[5]),
        pltpu.make_async_copy(quarter(pending.at[0], mine), p_buf.at[1], load_sem.at[6]),
    ]
    for copy in loads + p_loads:
        copy.start()

    barrier = pltpu.get_barrier_semaphore()
    for device in partner + [other_core, other_y]:
        pl.semaphore_signal(barrier, inc=1, device_id=device, device_id_type=MESH)
    pl.semaphore_wait(barrier, len(partner) + 2)

    def rows_of(offset):
        dz, dx, dy = offset
        return mp_at(z + 4 - dz, x + 4 - dx, yh + dy) * SHARD

    def index_of(offset):
        return (offset[0] * 4 + offset[1]) * 2 + offset[2]

    def place(item):
        first, rows = PIECES[item[0]][:2]
        return c_buf.at[pl.ds(pl.multiple_of(rows_of(item[1]) + first, 16), rows)]

    def remote(src, dst, ssem, rsem, device):
        return pltpu.make_async_remote_copy(src, dst, ssem, rsem, device_id=device, device_id_type=MESH)

    def passing(item, link):
        dst = place(item)
        first, rows = PIECES[item[0]][:2]
        src = cotangent.at[0, pl.ds(first, rows)] if item[1] == (0, 0, 0) else dst
        return remote(src, dst, send_sem.at[link], recv_sem.at[index_of(moved(item[1], link)), item[0]], partner[link])

    def landed(item):
        dst = place(item)
        remote(dst, dst, send_sem.at[0], recv_sem.at[index_of(item[1]), item[0]], partner[0]).wait_recv()

    swap = [
        remote(quarter(pending.at[0], half * 2 + 1 - core), pc_buf.at[half], isl_send.at[half], isl_recv.at[half], other_core)
        for half in (0, 1)
    ]
    for copy in swap:
        copy.start()
    to_y = remote(p_buf.at[0], py_buf, isl_send.at[2], isl_recv.at[2], other_y)
    fresh_y = remote(p_buf.at[1], quarter(fresh, mine), isl_send.at[3], isl_recv.at[3], other_y)
    fresh_c = remote(p_buf.at[1], quarter(fresh, mine), isl_send.at[4], isl_recv.at[4], other_core)
    relay_c = remote(quarter(fresh, theirs), quarter(fresh, theirs), isl_send.at[5], isl_recv.at[5], other_core)
    ng_out = pltpu.make_async_copy(g_buf, new_global, out_sem.at[8])
    nm_out = pltpu.make_async_copy(m_buf, new_momentum, out_sem.at[9])

    backward_scale = 1.0 / math.sqrt(D)
    blend = -mix_weight * inner_rate / math.sqrt(TOKENS)
    tile = 256

    def reduce():
        for copy in p_loads:
            copy.wait()
        for copy in swap:
            copy.wait()

        def step(i, _):
            rows = pl.ds(pl.multiple_of(i * tile, tile), tile)
            p_buf[0, rows] = (p_buf[0, rows].astype(jnp.float32) + pc_buf[1 - yl, rows].astype(jnp.float32)).astype(jnp.bfloat16)
            return 0

        lax.fori_loop(0, 1024 // tile, step, 0)
        to_y.start()

    def outer():
        loads[3].wait()
        loads[4].wait()
        to_y.wait()

        def step(i, _):
            rows = pl.ds(pl.multiple_of(i * tile, tile), tile)
            mean = (
                p_buf[1, rows].astype(jnp.float32) + pc_buf[yl, rows].astype(jnp.float32) + py_buf[rows].astype(jnp.float32)
            ) / islands
            momentum = decay_rate * m_buf[rows] + mean
            weight = g_buf[rows] - outer_rate * (mean + decay_rate * momentum)
            m_buf[rows] = momentum
            g_buf[rows] = weight
            p_buf[1, rows] = weight.astype(jnp.bfloat16)
            return 0

        lax.fori_loop(0, 1024 // tile, step, 0)
        fresh_y.start()
        fresh_c.start()
        ng_out.start()
        nm_out.start()

    def relay():
        fresh_y.wait()
        relay_c.start()

    def add_base(source, index):
        def step(i, _):
            rows = pl.ds(pl.multiple_of(i * tile, tile), tile)
            full = pl.ds(pl.multiple_of(index * 1024 + i * tile, tile), tile)
            base = mix_weight * w_buf[full].astype(jnp.float32) + (1.0 - mix_weight) * p_buf[source, rows].astype(jnp.float32)
            acc[full] += base * (1.0 / blend)
            return 0

        lax.fori_loop(0, 1024 // tile, step, 0)

    def blend_all():
        fresh_c.wait()
        relay_c.wait()
        add_base(1, mine)
        for index in (theirs, yl * 2 + 1 - core, (1 - yl) * 2 + 1 - core):
            load = pltpu.make_async_copy(quarter(fresh, index), p_buf.at[0], load_sem.at[7])
            load.start()
            load.wait()
            add_base(0, index)

    def pair_rows(pair):
        return pl.multiple_of(mp_at(z + 4 - pair[0], x + 4 - pair[1], 0) * SHARD, 2 * SHARD)

    hg_copies = []

    def hg(pair):
        first = pair_rows(pair)
        rows = pl.ds(first, 2 * SHARD)
        slot = len(hg_copies) % 2
        if len(hg_copies) == 0:
            loads[0].wait()
            loads[1].wait()
        if len(hg_copies) >= 2:
            hg_copies[-2].wait()
        block = jnp.dot(c_buf[rows], w_buf[...], preferred_element_type=jnp.float32) * backward_scale
        hg_buf[slot] = block.astype(jnp.bfloat16)
        copy = pltpu.make_async_copy(hg_buf.at[slot], hidden_grad.at[0, rows], hg_sem.at[slot])
        copy.start()
        hg_copies.append(copy)

    width = 512

    def product(first, i):
        columns = pl.ds(pl.multiple_of(i * width, width), width)
        rows = pl.ds(first, 2 * SHARD)
        return columns, lax.dot_general(
            c_buf[rows, columns], h_buf[rows], (((0,), (0,)), ((), ())), preferred_element_type=jnp.float32
        )

    def wg(pair, start):
        first = pair_rows(pair)
        if start:
            loads[2].wait()

        def step(i, _):
            columns, block = product(first, i)
            if start:
                acc[columns] = block
            else:
                acc[columns] += block
            return 0

        lax.fori_loop(0, D // width, step, 0)

    def end(pair):
        first = pair_rows(pair)

        def out(i):
            columns = pl.ds(pl.multiple_of(i * width, width), width)
            return pltpu.make_async_copy(w_buf.at[columns], merged.at[0, columns], out_sem.at[i])

        def step(i, _):
            columns, block = product(first, i)
            w_buf[columns] = ((acc[columns] + block) * blend).astype(jnp.bfloat16)
            out(i).start()
            return 0

        lax.fori_loop(0, D // width, step, 0)
        for i in range(D // width):
            out(i).wait()

    tasks = {"reduce": reduce, "outer": outer, "relay": relay, "blend": blend_all, "hg": hg, "wg": wg, "end": end}
    steps, sent_rows, _ = plan()
    for step in steps:
        if step[0] == "send":
            passing(*step[1:]).start()
        elif step[0] == "wait":
            landed(step[1])
        else:
            tasks[step[1]](*step[2:])
    for copy in hg_copies[-2:]:
        copy.wait()
    ng_out.wait()
    nm_out.wait()
    for link, rows in enumerate(sent_rows):
        whole = c_buf.at[pl.ds(0, rows)]
        remote(whole, whole, send_sem.at[link], recv_sem.at[0, 0], partner[link]).wait_send()


def body(hidden, cotangent, local_weight, pending, global_weight, outer_momentum):
    big = jax.ShapeDtypeStruct((1, D, FF_SHARE), jnp.bfloat16)
    part = jax.ShapeDtypeStruct((D // islands, FF_SHARE), jnp.float32)
    slots = jax.ShapeDtypeStruct((D, FF_SHARE), jnp.bfloat16)
    outs = pl.pallas_call(
        kernel,
        out_shape=(big, big, part, part, slots),
        in_specs=[pl.BlockSpec(memory_space=pl.ANY)] * 6,
        out_specs=[pl.BlockSpec(memory_space=pl.ANY)] * 5,
        scratch_shapes=[
            pltpu.VMEM((TOKENS, D), jnp.bfloat16),
            pltpu.VMEM((TOKENS, FF_SHARE), jnp.bfloat16),
            pltpu.VMEM((D, FF_SHARE), jnp.bfloat16),
            pltpu.VMEM((D, FF_SHARE), jnp.float32),
            pltpu.VMEM((2, 2 * SHARD, FF_SHARE), jnp.bfloat16),
            pltpu.VMEM((2, 1024, FF_SHARE), jnp.bfloat16),
            pltpu.VMEM((2, 1024, FF_SHARE), jnp.bfloat16),
            pltpu.VMEM((1024, FF_SHARE), jnp.bfloat16),
            pltpu.VMEM((1024, FF_SHARE), jnp.float32),
            pltpu.VMEM((1024, FF_SHARE), jnp.float32),
            pltpu.SemaphoreType.DMA((len(LINKS),)),
            pltpu.SemaphoreType.DMA((32, len(PIECES))),
            pltpu.SemaphoreType.DMA((8,)),
            pltpu.SemaphoreType.DMA((2,)),
            pltpu.SemaphoreType.DMA((10,)),
            pltpu.SemaphoreType.DMA((6,)),
            pltpu.SemaphoreType.DMA((6,)),
        ],
        compiler_params=pltpu.CompilerParams(collective_id=0, has_side_effects=True, vmem_limit_bytes=63 * MIB),
        cost_estimate=pl.CostEstimate(flops=4 * TOKENS * D * FF_SHARE, bytes_accessed=64 * MIB, transcendentals=0),
        name="gather_and_update",
    )(hidden, cotangent, local_weight, pending, global_weight, outer_momentum)
    return outs[:4]


def solution(mesh):
    placed = (
        P("island", None, "mp"),
        P("island", "mp", None),
        P("island", None, "mp"),
        P("island", None, "mp"),
        P("island", "mp"),
        P("island", "mp"),
    )
    return jax.shard_map(
        body,
        mesh=mesh,
        in_specs=placed,
        out_specs=(
            P("island", None, "mp"),
            P("island", None, "mp"),
            P("island", "mp"),
            P("island", "mp"),
        ),
        check_vma=False,
    )
```

time: 359 us -> 258 us (0.72); the launches traced: 359 us -> 254 us
  waiting for transfers between devices: 288 us -> 0 us
  Pallas kernels: 0 us -> 212 us
  matrix products: 49.5 us -> 0 us
  local copies, waits for them, and re-layouts: 0.01 us -> 41.3 us
  between operations: 15.5 us -> 0.65 us
  other arithmetic: 5.76 us -> 0 us
    pallas_call x0 -> x1, Pallas kernels: none -> 212 us  [body(): pl.pallas_call(kernel, out_shape=(big, big, part, part, slots), in_specs=...]
    all_gather x2 -> x0, waiting for transfers between devices: 171 us -> none  [the longest x1 152 us: body(): piece = lax.all_gather(grads_out, 'mp', axis=0, tiled=True)]
    psum x1 -> x0, waiting for transfers between devices: 115 us -> none  [body(): summed_all = lax.psum(pending[0], 'island').astype(jnp.float32)]
    dot_general x2 -> x0, matrix products: 49.5 us -> none  [the longest x1 25.9 us: body(): lax.dot_general(piece, activation, contract_tokens, preferred_element_typ...]
    unnamed x2 -> x13, local copies, waits for them, and re-layouts: 0.01 us -> 41.3 us
    convert_element_type x1 -> x0, other arithmetic: 5.76 us -> none  [body(): new_global.astype(jnp.bfloat16)]
  transfers between devices with their start and end apart: 3 -> 0, of which waited for: 3 -> 0; matrix products, arithmetic and copies ran while one was open for 8% -> 0% of each run, Pallas kernels for 0% -> 0%
where the time goes in v1:
time: 258 us; the launch traced here: 254 us
  Pallas kernels  212 us (82%)
  local copies, waits for them, and re-layouts  41.3 us (16%)
    pallas_call x1, Pallas kernels, body(): pl.pallas_call(kernel, out_shape=(big, big, part, part, slots), in_specs=...  212 us
    unnamed x13, local copies, waits for them, and re-layouts  41.3 us

profile of v1, /device:TPU:1, one launch (start us, length us, event | category | flops | bytes accessed | tf_op | source)
XLA Modules:
  0.0 253.6 jit_solution(10075577651499938788)
XLA Ops:
  0.6 0.0 copy-start.1
  0.6 3.0 %copy.13.global_weight = f32[1024,448]{1,0:T(8,128)} copy(f32[1024,448]{0,1:T(8,128)} %param.10) | data formatting | bytes 3670016 | tf_op args[4]
  3.6 0.0 copy-done.1
  3.6 1.8 copy.14.outer_momentum
  5.4 6.4 %copy.10.hidden = bf16[1,4096,448]{2,1,0:T(8,128)(2,1)} copy(bf16[1,4096,448]{1,2,0:T(8,128)(2,1)} %param.6) | data formatting | bytes 7340032 | tf_op args[0]
  11.8 6.5 %copy.11.local_weight = bf16[1,4096,448]{2,1,0:T(8,128)(2,1)} copy(bf16[1,4096,448]{1,2,0:T(8,128)(2,1)} %param.8) | data formatting | bytes 7340032 | tf_op args[2]
  18.3 6.4 %copy.12.pending = bf16[1,4096,448]{2,1,0:T(8,128)(2,1)} copy(bf16[1,4096,448]{1,2,0:T(8,128)(2,1)} %param.9) | data formatting | bytes 7340032 | tf_op args[3]
  24.7 211.7 %gather_and_update.1 = (bf16[1,4096,448]{2,1,0:T(8,128)(2,1)}, bf16[1,4096,448]{2,1,0:T(8,128)(2,1)}, f32[1024,448]{1,0:T(8,128)}, f32[1024,448]{1,0:T(8,128)}, bf16[4096,448]{1,0:T(8,128)(2,1)}) custom-call(bf16[1,4096,448]{2,1,0:T(8,128)(2,1)} %copy.10.hidden, bf16[1,128,4096]{2,1,0:T(8,128)(2,1)} %cotangent.1, bf16[1,4096,448]{2,1,0:T(8,128)(2,1)} %copy.11.local_weight, ...), custom_call_target="tpu_custom_call" | custom-call | flops 30064771072 | bytes 67108864 | tf_op jit(solution)/shard_map/gather_and_update/pallas_call | solution.py:385
  236.4 6.3 %copy.15 = bf16[1,4096,448]{1,2,0:T(8,128)(2,1)} copy(bf16[1,4096,448]{2,1,0:T(8,128)(2,1)} %get-tuple-element.12) | data formatting | bytes 7340032
  242.7 0.0 copy-start
  242.7 2.9 %copy.17 = f32[1024,448]{0,1:T(8,128)} copy(f32[1024,448]{1,0:T(8,128)} %get-tuple-element.14) | data formatting | bytes 3670016
  245.6 0.0 copy-done
  245.6 1.7 copy.18
  247.4 6.3 %copy.16 = bf16[1,4096,448]{1,2,0:T(8,128)(2,1)} copy(bf16[1,4096,448]{2,1,0:T(8,128)(2,1)} %get-tuple-element.13) | data formatting | bytes 7340032
Async XLA Ops:
  0.6 3.0 %copy-start.1 = (f32[1024,448]{0,1:T(8,128)S(1)}, f32[1024,448]{0,1:T(8,128)}, u32[]{:S(2)}) copy-start(f32[1024,448]{0,1:T(8,128)} %param.11) | copy-start | bytes 5505028
  242.7 3.0 %copy-start = (f32[1024,448]{1,0:T(8,128)S(1)}, f32[1024,448]{1,0:T(8,128)}, u32[]{:S(2)}) copy-start(f32[1024,448]{1,0:T(8,128)} %get-tuple-element.15) | copy-start | bytes 5505028

commit v2 on v1

--- a/solution.py
+++ b/solution.py
@@ -60,17 +60,27 @@
     return found
 
 
-def depth_of(piece, offset):
-    best = 0.0
+def order_of(pair):
+    dz, dx = min(pair[0], 4 - pair[0]), min(pair[1], 4 - pair[1])
+    return (dz + dx, max(dz, dx), pair)
+
+
+PAIRS = sorted(((dz, dx) for dz in range(4) for dx in range(4)), key=order_of)
+FIRST_DUE, LAST_DUE, HOP = 30.0, 150.0, 6.0
+
+
+def due_of(piece, offset):
+    rank = PAIRS.index(offset[:2])
+    best = FIRST_DUE + (LAST_DUE - FIRST_DUE) * rank / (len(PAIRS) - 1)
     for link in links_of(piece, offset):
-        best = max(best, 1.0 + depth_of(piece, moved(offset, link)))
+        best = min(best, due_of(piece, moved(offset, link)) - HOP)
     return best
 
 
 def plan():
     unit = 2.87 / 16
-    latency = 2.0
-    hg_time, wg_time = 2.2, 2.2
+    latency = LATENCY
+    hg_time, wg_time = TASK_TIMES
     heaps = [[] for _ in LINKS]
     free_at = [0.0] * len(LINKS)
     queued = [[] for _ in LINKS]
@@ -80,36 +90,42 @@
     now = 0.0
     sent_rows = [0] * len(LINKS)
     todo_hg, todo_wg = [], []
-    islands_due = [(8.0, "reduce"), (34.0, "outer"), (62.0, "relay"), (76.0, "blend")]
+    islands_due = [(ISLAND_AT, "reduce")]
+    island_rows = FF_SHARE // 4
     pieces = range(len(PIECES))
+    due = {}
+    finished = []
 
     def offer(item):
         for link in links_of(*item):
-            heaps[link].append((-depth_of(item[0], moved(item[1], link)), now, item))
+            after = (item[0], moved(item[1], link))
+            if after not in due:
+                due[after] = due_of(*after)
+            heaps[link].append((due[after], item))
 
     def pump():
         for link in range(len(LINKS)):
             while True:
                 queued[link] = [t for t in queued[link] if t > now]
-                if len(queued[link]) >= 3 or not heaps[link]:
+                if len(queued[link]) >= DEPTH or not heaps[link]:
                     break
                 heaps[link].sort()
-                _, _, item = heaps[link].pop(0)
+                _, item = heaps[link].pop(0)
                 rows = PIECES[item[0]][1]
                 start = max(now, free_at[link])
                 free_at[link] = start + unit * rows
                 queued[link].append(free_at[link])
                 sent_rows[link] += rows
                 steps.append(("send", item, link))
-                arrivals.append((free_at[link] + latency, (item[0], moved(item[1], link))))
+                arrivals.append((free_at[link] + latency[link], (item[0], moved(item[1], link))))
 
     def land(item):
         have[item] = True
-        offset = item[1]
-        pair = offset[:2]
+        pair = item[1][:2]
         if all((p, pair + (dy,)) in have for p in pieces for dy in (0, 1)):
             todo_hg.append(pair)
             todo_wg.append(pair)
+            finished.append((round(now, 1), pair))
 
     for p in pieces:
         item = (p, (0, 0, 0))
@@ -128,8 +144,15 @@
             now += 0.06
         pump()
         if islands_due and islands_due[0][0] <= now and not (islands_due[0][1] == "blend" and first_wg):
-            steps.append(("task", islands_due.pop(0)[1]))
-            now += 4.0
+            name = islands_due.pop(0)[1]
+            steps.append(("task", name))
+            now += 1.5
+            if name in ("reduce", "outer"):
+                free_at[4] = max(now, free_at[4]) + unit * island_rows
+                queued[4].append(free_at[4])
+                islands_due.append((free_at[4] + latency[4], "outer" if name == "reduce" else "relay"))
+            elif name == "relay":
+                islands_due.append((now + 12.0, "blend"))
         elif todo_hg and len(todo_hg) >= len(todo_wg):
             steps.append(("task", "hg", todo_hg.pop(0)))
             now += hg_time
@@ -139,14 +162,20 @@
             now += wg_time
         else:
             times = [t for t, _ in arrivals[:1]] + [t for t, _ in islands_due[:1]]
-            for q in queued:
-                if len(q) >= 3:
+            for link, q in enumerate(queued):
+                if len(q) >= DEPTH and heaps[link]:
                     times.append(min(q))
             times = [t for t in times if t > now]
             now = min(times) if times else now + 0.1
     last = max(i for i, s in enumerate(steps) if s[0] == "task" and s[1] == "wg")
     steps[last] = ("task", "end") + steps[last][2:3]
-    return steps, sent_rows, now
+    return steps, sent_rows, now, finished
+
+
+TASK_TIMES = (1.5, 1.5)
+DEPTH = 2
+LATENCY = (4.0, 4.0, 4.0, 4.0, 6.0)
+ISLAND_AT = 16.0
 
 
 def kernel(
@@ -174,20 +203,20 @@
     other_y = {"island": (1 - yl) * 2 + core}
 
     loads = [
-        pltpu.make_async_copy(cotangent.at[0], c_buf.at[pl.ds(pl.multiple_of(mp * SHARD, SHARD), SHARD)], load_sem.at[0]),
-        pltpu.make_async_copy(local_weight.at[0], w_buf, load_sem.at[1]),
-        pltpu.make_async_copy(hidden.at[0], h_buf, load_sem.at[2]),
+        pltpu.make_async_copy(cotangent, c_buf.at[pl.ds(pl.multiple_of(mp * SHARD, SHARD), SHARD)], load_sem.at[0]),
+        pltpu.make_async_copy(local_weight, w_buf, load_sem.at[1]),
+        pltpu.make_async_copy(hidden, h_buf, load_sem.at[2]),
         pltpu.make_async_copy(global_weight, g_buf, load_sem.at[3]),
         pltpu.make_async_copy(outer_momentum, m_buf, load_sem.at[4]),
     ]
 
     def quarter(ref, index):
-        return ref.at[pl.ds(pl.multiple_of(index * 1024, 1024), 1024)]
+        return ref.at[:, pl.ds(pl.multiple_of(index * 1024, 1024), 1024)]
 
     mine, theirs = yl * 2 + core, (1 - yl) * 2 + core
     p_loads = [
-        pltpu.make_async_copy(quarter(pending.at[0], theirs), p_buf.at[0], load_sem.at[5]),
-        pltpu.make_async_copy(quarter(pending.at[0], mine), p_buf.at[1], load_sem.at[6]),
+        pltpu.make_async_copy(quarter(pending, theirs), p_buf.at[0], load_sem.at[5]),
+        pltpu.make_async_copy(quarter(pending, mine), p_buf.at[1], load_sem.at[6]),
     ]
     for copy in loads + p_loads:
         copy.start()
@@ -214,7 +243,7 @@
     def passing(item, link):
         dst = place(item)
         first, rows = PIECES[item[0]][:2]
-        src = cotangent.at[0, pl.ds(first, rows)] if item[1] == (0, 0, 0) else dst
+        src = cotangent.at[pl.ds(first, rows)] if item[1] == (0, 0, 0) else dst
         return remote(src, dst, send_sem.at[link], recv_sem.at[index_of(moved(item[1], link)), item[0]], partner[link])
 
     def landed(item):
@@ -222,7 +251,7 @@
         remote(dst, dst, send_sem.at[0], recv_sem.at[index_of(item[1]), item[0]], partner[0]).wait_recv()
 
     swap = [
-        remote(quarter(pending.at[0], half * 2 + 1 - core), pc_buf.at[half], isl_send.at[half], isl_recv.at[half], other_core)
+        remote(quarter(pending, half * 2 + 1 - core), pc_buf.at[half], isl_send.at[half], isl_recv.at[half], other_core)
         for half in (0, 1)
     ]
     for copy in swap:
@@ -236,7 +265,7 @@
 
     backward_scale = 1.0 / math.sqrt(D)
     blend = -mix_weight * inner_rate / math.sqrt(TOKENS)
-    tile = 256
+    tile = 64
 
     def reduce():
         for copy in p_loads:
@@ -249,7 +278,7 @@
             p_buf[0, rows] = (p_buf[0, rows].astype(jnp.float32) + pc_buf[1 - yl, rows].astype(jnp.float32)).astype(jnp.bfloat16)
             return 0
 
-        lax.fori_loop(0, 1024 // tile, step, 0)
+        lax.fori_loop(0, FF_SHARE // tile, step, 0)
         to_y.start()
 
     def outer():
@@ -269,7 +298,7 @@
             p_buf[1, rows] = weight.astype(jnp.bfloat16)
             return 0
 
-        lax.fori_loop(0, 1024 // tile, step, 0)
+        lax.fori_loop(0, FF_SHARE // tile, step, 0)
         fresh_y.start()
         fresh_c.start()
         ng_out.start()
@@ -280,14 +309,17 @@
         relay_c.start()
 
     def add_base(source, index):
+        columns = pl.ds(pl.multiple_of(index * 1024, 1024), 1024)
+
         def step(i, _):
             rows = pl.ds(pl.multiple_of(i * tile, tile), tile)
-            full = pl.ds(pl.multiple_of(index * 1024 + i * tile, tile), tile)
-            base = mix_weight * w_buf[full].astype(jnp.float32) + (1.0 - mix_weight) * p_buf[source, rows].astype(jnp.float32)
-            acc[full] += base * (1.0 / blend)
+            base = mix_weight * w_buf[rows, columns].astype(jnp.float32) + (1.0 - mix_weight) * p_buf[source, rows].astype(
+                jnp.float32
+            )
+            acc[rows, columns] += base * (1.0 / blend)
             return 0
 
-        lax.fori_loop(0, 1024 // tile, step, 0)
+        lax.fori_loop(0, FF_SHARE // tile, step, 0)
 
     def blend_all():
         fresh_c.wait()
@@ -299,60 +331,58 @@
             load.wait()
             add_base(0, index)
 
-    def pair_rows(pair):
-        return pl.multiple_of(mp_at(z + 4 - pair[0], x + 4 - pair[1], 0) * SHARD, 2 * SHARD)
+    def pair_tokens(pair):
+        return pl.ds(pl.multiple_of(mp_at(z + 4 - pair[0], x + 4 - pair[1], 0) * SHARD, 2 * SHARD), 2 * SHARD)
 
     hg_copies = []
 
     def hg(pair):
-        first = pair_rows(pair)
-        rows = pl.ds(first, 2 * SHARD)
+        tokens = pair_tokens(pair)
         slot = len(hg_copies) % 2
         if len(hg_copies) == 0:
             loads[0].wait()
             loads[1].wait()
         if len(hg_copies) >= 2:
             hg_copies[-2].wait()
-        block = jnp.dot(c_buf[rows], w_buf[...], preferred_element_type=jnp.float32) * backward_scale
-        hg_buf[slot] = block.astype(jnp.bfloat16)
-        copy = pltpu.make_async_copy(hg_buf.at[slot], hidden_grad.at[0, rows], hg_sem.at[slot])
+        block = lax.dot_general(
+            w_buf[...], c_buf[tokens], (((1,), (1,)), ((), ())), preferred_element_type=jnp.float32
+        )
+        hg_buf[slot] = (block * backward_scale).astype(jnp.bfloat16)
+        copy = pltpu.make_async_copy(hg_buf.at[slot], hidden_grad.at[:, tokens], hg_sem.at[slot])
         copy.start()
         hg_copies.append(copy)
 
     width = 512
 
-    def product(first, i):
+    def product(tokens, i):
         columns = pl.ds(pl.multiple_of(i * width, width), width)
-        rows = pl.ds(first, 2 * SHARD)
-        return columns, lax.dot_general(
-            c_buf[rows, columns], h_buf[rows], (((0,), (0,)), ((), ())), preferred_element_type=jnp.float32
-        )
+        return columns, jnp.dot(h_buf[:, tokens], c_buf[tokens, columns], preferred_element_type=jnp.float32)
 
     def wg(pair, start):
-        first = pair_rows(pair)
+        tokens = pair_tokens(pair)
         if start:
             loads[2].wait()
 
         def step(i, _):
-            columns, block = product(first, i)
+            columns, block = product(tokens, i)
             if start:
-                acc[columns] = block
+                acc[:, columns] = block
             else:
-                acc[columns] += block
+                acc[:, columns] += block
             return 0
 
         lax.fori_loop(0, D // width, step, 0)
 
     def end(pair):
-        first = pair_rows(pair)
+        tokens = pair_tokens(pair)
 
         def out(i):
             columns = pl.ds(pl.multiple_of(i * width, width), width)
-            return pltpu.make_async_copy(w_buf.at[columns], merged.at[0, columns], out_sem.at[i])
+            return pltpu.make_async_copy(w_buf.at[:, columns], merged.at[:, columns], out_sem.at[i])
 
         def step(i, _):
-            columns, block = product(first, i)
-            w_buf[columns] = ((acc[columns] + block) * blend).astype(jnp.bfloat16)
+            columns, block = product(tokens, i)
+            w_buf[:, columns] = ((acc[:, columns] + block) * blend).astype(jnp.bfloat16)
             out(i).start()
             return 0
 
@@ -361,7 +391,7 @@
             out(i).wait()
 
     tasks = {"reduce": reduce, "outer": outer, "relay": relay, "blend": blend_all, "hg": hg, "wg": wg, "end": end}
-    steps, sent_rows, _ = plan()
+    steps, sent_rows = plan()[:2]
     for step in steps:
         if step[0] == "send":
             passing(*step[1:]).start()
@@ -379,25 +409,24 @@
 
 
 def body(hidden, cotangent, local_weight, pending, global_weight, outer_momentum):
-    big = jax.ShapeDtypeStruct((1, D, FF_SHARE), jnp.bfloat16)
-    part = jax.ShapeDtypeStruct((D // islands, FF_SHARE), jnp.float32)
-    slots = jax.ShapeDtypeStruct((D, FF_SHARE), jnp.bfloat16)
+    big = jax.ShapeDtypeStruct((FF_SHARE, D), jnp.bfloat16)
+    part = jax.ShapeDtypeStruct((FF_SHARE, D // islands), jnp.float32)
     outs = pl.pallas_call(
         kernel,
-        out_shape=(big, big, part, part, slots),
+        out_shape=(big, big, part, part, big),
         in_specs=[pl.BlockSpec(memory_space=pl.ANY)] * 6,
         out_specs=[pl.BlockSpec(memory_space=pl.ANY)] * 5,
         scratch_shapes=[
             pltpu.VMEM((TOKENS, D), jnp.bfloat16),
-            pltpu.VMEM((TOKENS, FF_SHARE), jnp.bfloat16),
-            pltpu.VMEM((D, FF_SHARE), jnp.bfloat16),
-            pltpu.VMEM((D, FF_SHARE), jnp.float32),
-            pltpu.VMEM((2, 2 * SHARD, FF_SHARE), jnp.bfloat16),
-            pltpu.VMEM((2, 1024, FF_SHARE), jnp.bfloat16),
-            pltpu.VMEM((2, 1024, FF_SHARE), jnp.bfloat16),
-            pltpu.VMEM((1024, FF_SHARE), jnp.bfloat16),
-            pltpu.VMEM((1024, FF_SHARE), jnp.float32),
-            pltpu.VMEM((1024, FF_SHARE), jnp.float32),
+            pltpu.VMEM((FF_SHARE, TOKENS), jnp.bfloat16),
+            pltpu.VMEM((FF_SHARE, D), jnp.bfloat16),
+            pltpu.VMEM((FF_SHARE, D), jnp.float32),
+            pltpu.VMEM((2, FF_SHARE, 2 * SHARD), jnp.bfloat16),
+            pltpu.VMEM((2, FF_SHARE, 1024), jnp.bfloat16),
+            pltpu.VMEM((2, FF_SHARE, 1024), jnp.bfloat16),
+            pltpu.VMEM((FF_SHARE, 1024), jnp.bfloat16),
+            pltpu.VMEM((FF_SHARE, 1024), jnp.float32),
+            pltpu.VMEM((FF_SHARE, 1024), jnp.float32),
             pltpu.SemaphoreType.DMA((len(LINKS),)),
             pltpu.SemaphoreType.DMA((32, len(PIECES))),
             pltpu.SemaphoreType.DMA((8,)),
@@ -406,11 +435,11 @@
             pltpu.SemaphoreType.DMA((6,)),
             pltpu.SemaphoreType.DMA((6,)),
         ],
-        compiler_params=pltpu.CompilerParams(collective_id=0, has_side_effects=True, vmem_limit_bytes=63 * MIB),
+        compiler_params=pltpu.CompilerParams(collective_id=0, has_side_effects=True, vmem_limit_bytes=62 * MIB),
         cost_estimate=pl.CostEstimate(flops=4 * TOKENS * D * FF_SHARE, bytes_accessed=64 * MIB, transcendentals=0),
         name="gather_and_update",
-    )(hidden, cotangent, local_weight, pending, global_weight, outer_momentum)
-    return outs[:4]
+    )(hidden[0].T, cotangent[0], local_weight[0].T, pending[0].T, global_weight.T, outer_momentum.T)
+    return outs[0].T[None], outs[1].T[None], outs[2].T, outs[3].T
 
 
 def solution(mesh):

time: 258 us -> 175 us (0.68); the launches traced: 254 us -> 174 us
  Pallas kernels: 212 us -> 163 us
  local copies, waits for them, and re-layouts: 41.3 us -> 10.7 us
    pallas_call x1, Pallas kernels: 212 us -> 163 us  [body(): pl.pallas_call(kernel, out_shape=(big, big, part, part, big), in_specs=[p...]
    unnamed x13 -> x10, local copies, waits for them, and re-layouts: 41.3 us -> 10.7 us
where the time goes in v2:
time: 175 us; the launch traced here: 174 us
  Pallas kernels  163 us (93%)
  local copies, waits for them, and re-layouts  10.7 us (6%)
    pallas_call x1, Pallas kernels, body(): pl.pallas_call(kernel, out_shape=(big, big, part, part, big), in_specs=[p...  163 us
    unnamed x10, local copies, waits for them, and re-layouts  10.7 us

profile of v2, /device:TPU:1, one launch (start us, length us, event | category | flops | bytes accessed | tf_op | source)
XLA Modules:
  0.0 174.5 jit_solution(3557669757135764770)
XLA Ops:
  0.6 163.2 %gather_and_update.1 = (bf16[448,4096]{1,0:T(8,128)(2,1)}, bf16[448,4096]{1,0:T(8,128)(2,1)}, f32[448,1024]{1,0:T(8,128)}, f32[448,1024]{1,0:T(8,128)}, bf16[448,4096]{1,0:T(8,128)(2,1)}) custom-call(bf16[448,4096]{1,0:T(8,128)(2,1)} %bitcast.24, bf16[128,4096]{1,0:T(8,128)(2,1)} %bitcast.29, bf16[448,4096]{1,0:T(8,128)(2,1)} %bitcast.25, ...), custom_call_target="tpu_custom_call" | custom-call | flops 30064771072 | bytes 67108864 | tf_op jit(solution)/shard_map/gather_and_update/pallas_call | solution.py:414
  163.8 0.0 copy-start
  163.8 4.4 %copy.14 = bf16[1,4096,448]{1,2,0:T(8,128)(2,1)} copy(bf16[1,4096,448]{1,2,0:T(8,128)(2,1)} %bitcast.21) | data formatting | bytes 7340032
  168.3 0.0 copy-done
  168.3 0.0 copy-start.2
  168.3 1.9 %copy.15 = bf16[1,4096,448]{1,2,0:T(8,128)(2,1)} copy(bf16[1,4096,448]{1,2,0:T(8,128)(2,1)S(1)} %bitcast.20) | data formatting | bytes 7340032
  170.1 1.0 copy-done.2
  171.1 0.0 copy-start.1
  171.1 1.2 copy.16
  172.3 0.9 copy-done.1
  173.2 1.2 copy.17
Async XLA Ops:
  163.8 4.5 %copy-start = (bf16[448,4096]{1,0:T(8,128)(2,1)S(1)}, bf16[448,4096]{1,0:T(8,128)(2,1)}, u32[]{:S(2)}) copy-start(bf16[448,4096]{1,0:T(8,128)(2,1)} %get-tuple-element.9) | copy-start | bytes 11010052
  168.3 2.8 %copy-start.2 = (f32[448,1024]{1,0:T(8,128)S(1)}, f32[448,1024]{1,0:T(8,128)}, u32[]{:S(2)}) copy-start(f32[448,1024]{1,0:T(8,128)} %get-tuple-element.10) | copy-start | bytes 5505028
  171.1 2.2 %copy-start.1 = (f32[448,1024]{1,0:T(8,128)S(1)}, f32[448,1024]{1,0:T(8,128)}, u32[]{:S(2)}) copy-start(f32[448,1024]{1,0:T(8,128)} %get-tuple-element.11) | copy-start | bytes 5505028

commit v3 on v0

v3 whole, which is shorter than its diff:
```python
import math

import jax
import jax.numpy as jnp
from jax import lax
from jax.experimental import pallas as pl
from jax.experimental.pallas import tpu as pltpu
from jax.sharding import PartitionSpec as P

D = 4096
TOKENS = 4096
FF_SHARE = 448
SHARD = 128
HALF = FF_SHARE // 2
CUT = 2048

inner_rate = 0.3
outer_rate = 0.7
decay_rate = 0.9
mix_weight = 0.5
islands = 4

MESH = pl.DeviceIdType.MESH
MIB = 2**20

KINDS = (((0, 64), (0, 0)), ((0, 32), (32, 32)))
SPANS = ((0, CUT), (CUT, D - CUT))
LINKS = ((0, 1), (0, -1), (1, 2), (2, 1))
WRAP = (4, 4, 2)
ORIGIN = (0, 0, 0)
OFFSETS = tuple((dz, dx, dy) for dz in range(4) for dx in range(4) for dy in range(2))


def moved(offset, link):
    axis, step = LINKS[link]
    out = list(offset)
    out[axis] = (out[axis] + step) % WRAP[axis]
    return tuple(out)


def links_of(kind, offset):
    dz, dx, dy = offset
    found = []
    if offset == ORIGIN:
        found.append(2)
    if kind == 0 and dz == 0 and dy == 0:
        found.append(3)
    if kind == 1 and dy == 0:
        found.append(3)
    if kind == 0 or dy == 0:
        way = 1 if (dx + dy) % 2 == 0 else -1
        if dz == 0 or (dz == 1 and way == 1):
            found.append(0)
        if dz == 0 or (dz == 3 and way == -1):
            found.append(1)
    return found


def order_of(pair):
    dz, dx = min(pair[0], 4 - pair[0]), min(pair[1], 4 - pair[1])
    return (dz, dx, pair)


PAIRS = sorted(((dz, dx) for dz in range(4) for dx in range(4)), key=order_of)
DUE = ((24.0, 65.8), (59.8, 72.9))
HOP = 3.0
ORDER = ("hg0", "wg0", "hg1", "wg1")
TASK_TIMES = ((1.0, 0.83), (1.15, 0.83))
DEPTH = 2
LATENCY = (4.0, 4.0, 5.0, 6.0)
ISLAND_AT = 7.0
SWAP_AT = (18.0, 36.0)
WORK_AT = (46.0, 64.0)
SPECIAL_AT = (18.0, 26.0)


def due_of(span, kind, offset):
    first, last = DUE[span]
    best = first + (last - first) * PAIRS.index(offset[:2]) / (len(PAIRS) - 1)
    for link in links_of(kind, offset):
        best = min(best, due_of(span, kind, moved(offset, link)) - HOP)
    return best


def plan():
    per_kib = 22.4 / 1024
    heaps = [[] for _ in LINKS]
    free_at = [0.0, 0.0, 8.0, 0.0]
    queued = [[] for _ in LINKS]
    arrivals = []
    steps = []
    have = set()
    sent_rows = [[0, 0] for _ in LINKS]
    state = {"now": 0.0}
    todo = {"hg0": [], "wg0": [], "hg1": [], "wg1": []}
    done = {"hg0": set(), "wg0": set(), "hg1": set(), "wg1": set()}
    flags = set()
    due_tasks = [(SWAP_AT[0], "swap_w"), (SWAP_AT[1], "swap_h"), (ISLAND_AT, "reduce")]
    island_kib = FF_SHARE * 2
    finished = []

    def offer(span, kind, offset):
        for link in links_of(kind, offset) if KINDS[span][kind][1] else ():
            heaps[link].append((due_of(span, kind, moved(offset, link)), span, kind, offset))

    def pump():
        now = state["now"]
        for link in range(len(LINKS)):
            while True:
                queued[link] = [t for t in queued[link] if t > now]
                if len(queued[link]) >= DEPTH or not heaps[link]:
                    break
                heaps[link].sort()
                _, span, kind, offset = heaps[link].pop(0)
                rows = KINDS[span][kind][1]
                start = max(now, free_at[link])
                free_at[link] = start + per_kib * rows * SPANS[span][1] / 512
                queued[link].append(free_at[link])
                sent_rows[link][span] += rows
                steps.append(("send", span, kind, offset, link))
                arrivals.append((free_at[link] + LATENCY[link], "wait", span, kind, moved(offset, link)))

    def check(span, offset):
        pair = offset[:2]
        if all((w, span, k, pair + (dy,)) in have for w in ("wait", "other") for k in (0, 1) for dy in (0, 1)):
            todo[f"hg{span}"].append(pair)
            todo[f"wg{span}"].append(pair)
            finished.append((round(state["now"], 1), span, pair))

    def land(entry):
        _, what, span, kind, offset = entry
        state["now"] += 0.06
        if what == "other":
            steps.append(("other", span, offset))
            have.update({("other", span, 0, offset), ("other", span, 1, offset)})
        else:
            steps.append(("wait", span, kind, offset))
            have.add(("wait", span, kind, offset))
            if not KINDS[span][1 - kind][1]:
                have.add(("wait", span, 1 - kind, offset))
            offer(span, kind, offset)
            if ("wait", span, 1 - kind, offset) in have:
                steps.append(("across", span, offset))
                arrivals.append((state["now"] + 4.0, "other", span, 0, offset))
        check(span, offset)

    for span in (0, 1):
        steps.append(("seed", span))
        for kind in (0, 1):
            have.update({("wait", span, kind, ORIGIN), ("other", span, kind, ORIGIN)})
            offer(span, kind, ORIGIN)
            for dx in (1, 3) if KINDS[span][kind][1] else ():
                arrivals.append((SPECIAL_AT[span], "wait", span, kind, (0, dx, 0)))
    pump()
    total = 2 * 2 * 2 * 32
    while True:
        arrivals.sort()
        while arrivals and arrivals[0][0] <= state["now"]:
            land(arrivals.pop(0))
            arrivals.sort()
        pump()
        due_tasks.sort()
        now = state["now"]
        ready = None
        for name in ORDER:
            if now < WORK_AT[name[0] == "w"] or not todo[name]:
                continue
            options = [p for p in todo[name] if name != "hg1" or p in done["hg0"]]
            if name[0] == "w":
                options = [p for p in options if p in done["h" + name[1:]]]
            if options:
                ready = (name, options[0])
                break
        if due_tasks and due_tasks[0][0] <= now and not (due_tasks[0][1] == "blend" and not done["wg0"]):
            name = due_tasks.pop(0)[1]
            steps.append(("task", name) + ((len(done["wg1"]) > 0,) if name == "blend" else ()))
            flags.add(name)
            state["now"] += 1.5
            if name in ("reduce", "outer"):
                free_at[3] = max(state["now"], free_at[3]) + per_kib * island_kib
                queued[3].append(free_at[3])
                due_tasks.append((free_at[3] + LATENCY[3], "outer" if name == "reduce" else "relay"))
            elif name == "relay":
                due_tasks.append((state["now"] + 8.0, "lend"))
            elif name == "lend":
                due_tasks.append((max(state["now"] + 26.0, WORK_AT[1] + 4.0), "blend"))
        elif len(done["wg0"]) == len(PAIRS) and "blend" in flags and "end0" not in flags:
            steps.append(("task", "end0"))
            flags.add("end0")
            state["now"] += 2.0
        elif ready:
            name, pair = ready
            took = options[:2] if name[0] == "w" else pair
            steps.append(("task", name[:2], int(name[2]), took, not done[name] and not (name == "wg1" and "blend" in flags)))
            for one in took if name[0] == "w" else [pair]:
                todo[name].remove(one)
                done[name].add(one)
                state["now"] += TASK_TIMES[int(name[2])][name[0] == "w"]
        elif len(have) == total and len(done["wg1"]) == len(PAIRS) and not due_tasks:
            break
        else:
            times = [t[0] for t in arrivals[:1]] + [t[0] for t in due_tasks]
            for link, q in enumerate(queued):
                if len(q) >= DEPTH and heaps[link]:
                    times.append(min(q))
            times = [t for t in times if t > now]
            state["now"] = min(times) if times else now + 0.1
            if len(have) == total and len(done["wg1"]) == len(PAIRS):
                break
    while due_tasks:
        steps.append(("task", due_tasks.pop(0)[1]))
    last = max(i for i, s in enumerate(steps) if s[0] == "task" and s[1] == "wg")
    steps[last] = ("task", "end1", steps[last][3])
    return steps, sent_rows, state["now"], finished


def kernel(
    hidden, cotangent, local_weight, pending, global_weight, outer_momentum,
    hidden_grad, merged, new_global, new_momentum, fresh, lent,
    c_lo, c_hi, h_buf, w_buf, acc, part, p_buf, pc_buf, py_buf, g_buf, m_buf,
    send_sem, mine_sem, across_sem, other_sem, seed_sem, special_sem, swap_send, swap_recv,
    load_sem, hg_sem, hg_send, hg_recv, out_sem, back_send, back_recv, isl_send, isl_recv,
):
    island = lax.axis_index("island")
    mp = lax.axis_index("mp")
    z, x, yh = mp // 8, (mp // 2) % 4, mp % 2
    core, yl = island % 2, island // 2
    role = lax.rem(core + x, 2)
    c_bufs = (c_lo, c_hi)

    def mp_at(pz, px, py):
        return (lax.rem(pz, 4) * 4 + lax.rem(px, 4)) * 2 + lax.rem(py, 2)

    partner = [
        {"mp": mp_at(z + 1, x, yh)},
        {"mp": mp_at(z + 3, x, yh)},
        {"mp": mp_at(z, x + 2, yh)},
        {"mp": mp_at(z, x, yh + 1)},
    ]
    other_core = {"island": yl * 2 + 1 - core}
    other_y = {"island": (1 - yl) * 2 + core}

    def beside(step, its_role):
        return {"island": yl * 2 + lax.rem(x + 1 + its_role, 2), "mp": mp_at(z, x + step, yh)}

    def only(which, action):
        pl.when(role == which)(action)

    def remote(src, dst, ssem, rsem, device):
        return pltpu.make_async_remote_copy(src, dst, ssem, rsem, device_id=device, device_id_type=MESH)

    def quarter(ref, index):
        return ref.at[:, pl.ds(pl.multiple_of(index * 1024, 1024), 1024)]

    def half(index):
        return pl.ds(index * HALF, HALF)

    own = [
        pltpu.make_async_copy(
            cotangent.at[:, pl.ds(*SPANS[span])],
            c_bufs[span].at[pl.ds(pl.multiple_of(mp * SHARD, SHARD), SHARD)],
            load_sem.at[span],
        )
        for span in (0, 1)
    ]
    w_load = pltpu.make_async_copy(local_weight, w_buf, load_sem.at[2])
    h_load = pltpu.make_async_copy(hidden, h_buf, load_sem.at[3])
    g_load = pltpu.make_async_copy(global_weight, g_buf, load_sem.at[4])
    m_load = pltpu.make_async_copy(outer_momentum, m_buf, load_sem.at[5])
    mine, theirs = yl * 2 + core, (1 - yl) * 2 + core
    p_loads = [
        pltpu.make_async_copy(quarter(pending, theirs), p_buf.at[0], load_sem.at[6]),
        pltpu.make_async_copy(quarter(pending, mine), p_buf.at[1], load_sem.at[7]),
    ]

    @pl.when(role == 0)
    def _():
        for copy in own + [w_load, h_load]:
            copy.start()

    for copy in p_loads + [g_load, m_load]:
        copy.start()

    barrier = pltpu.get_barrier_semaphore()
    greeted = partner + [other_core, other_y] + [beside(step, r) for step in (1, 3) for r in (0, 1)]
    for device in greeted:
        pl.semaphore_signal(barrier, inc=1, device_id=device, device_id_type=MESH)
    pl.semaphore_wait(barrier, len(greeted))

    def index_of(offset):
        return (offset[0] * 4 + offset[1]) * 2 + offset[2]

    def rows_of(offset):
        dz, dx, dy = offset
        return mp_at(z + 4 - dz, x + 4 - dx, yh + dy) * SHARD

    def place(span, kind, offset, side):
        first, rows = KINDS[span][kind]
        return c_bufs[span].at[pl.ds(pl.multiple_of(rows_of(offset) + side * 64 + first, 16), rows)]

    def place_all(span, offset, side):
        return c_bufs[span].at[pl.ds(pl.multiple_of(rows_of(offset) + side * 64, 16), 64)]

    def send(span, kind, offset, link):
        ref = place(span, kind, offset, role)
        remote(
            ref, ref, send_sem.at[link, span], mine_sem.at[span, kind, index_of(moved(offset, link))], partner[link]
        ).start()

    def wait(span, kind, offset):
        ref = place(span, kind, offset, role)
        remote(ref, ref, send_sem.at[0, span], mine_sem.at[span, kind, index_of(offset)], partner[0]).wait_recv()

    def across(span, offset):
        ref = place_all(span, offset, role)
        remote(ref, ref, across_sem.at[span], other_sem.at[span, index_of(offset)], other_core).start()

    def other(span, offset):
        ref = place_all(span, offset, 1 - role)
        remote(ref, ref, across_sem.at[span], other_sem.at[span, index_of(offset)], other_core).wait_recv()

    def seed_copy(span):
        ref = c_bufs[span].at[pl.ds(pl.multiple_of(mp * SHARD, SHARD), SHARD)]
        return remote(ref, ref, seed_sem.at[0, span], seed_sem.at[1, span], other_core)

    def specials(span):
        for kind in (0, 1):
            first, rows = KINDS[span][kind]
            if not rows:
                continue
            for side in (0, 1):
                src = cotangent.at[pl.ds(side * 64 + first, rows), pl.ds(*SPANS[span])]
                dst = place(span, kind, ORIGIN, side)
                for step in (1, 3):
                    remote(
                        src, dst, special_sem.at[span], mine_sem.at[span, kind, index_of((0, step, 0))], beside(step, side)
                    ).start()

    def seed(span):
        @pl.when(role == 0)
        def _():
            own[span].wait()
            seed_copy(span).start()

        @pl.when(role == 1)
        def _():
            specials(span)
            seed_copy(span).wait_recv()

    swaps = [
        remote(source.at[half(i)], target.at[half(i)], swap_send.at[j, i], swap_recv.at[j, i], beside((1, 3)[i], 1))
        for j, (source, target) in enumerate(((local_weight, w_buf), (hidden, h_buf)))
        for i in (0, 1)
    ]

    def swap(which):
        @pl.when(role == 1)
        def _():
            for copy in swaps[2 * which : 2 * which + 2]:
                copy.start()

    pair_sum = [
        remote(quarter(pending, i * 2 + 1 - core), pc_buf.at[i], isl_send.at[i], isl_recv.at[i], other_core) for i in (0, 1)
    ]
    for copy in pair_sum:
        copy.start()
    to_y = remote(p_buf.at[0], py_buf, isl_send.at[2], isl_recv.at[2], other_y)
    fresh_y = remote(p_buf.at[1], quarter(fresh, mine), isl_send.at[3], isl_recv.at[3], other_y)
    fresh_c = remote(p_buf.at[1], quarter(fresh, mine), isl_send.at[4], isl_recv.at[4], other_core)
    relay_c = remote(quarter(fresh, theirs), quarter(fresh, theirs), isl_send.at[5], isl_recv.at[5], other_core)
    fresh_own = pltpu.make_async_copy(p_buf.at[1], quarter(fresh, mine), out_sem.at[4])
    ng_out = pltpu.make_async_copy(g_buf, new_global, out_sem.at[0])
    nm_out = pltpu.make_async_copy(m_buf, new_momentum, out_sem.at[1])

    backward_scale = 1.0 / math.sqrt(D)
    blend = -mix_weight * inner_rate / math.sqrt(TOKENS)
    tile = 64

    def by_tile(step):
        def one(i, _):
            step(pl.ds(pl.multiple_of(i * tile, tile), tile))
            return 0

        lax.fori_loop(0, FF_SHARE // tile, one, 0)

    def wide(value):
        return value.astype(jnp.float32)

    def reduce():
        for copy in p_loads + pair_sum:
            copy.wait()

        def step(rows):
            p_buf[0, rows] = (wide(p_buf[0, rows]) + wide(pc_buf[1 - yl, rows])).astype(jnp.bfloat16)

        by_tile(step)
        to_y.start()

    def outer():
        g_load.wait()
        m_load.wait()
        to_y.wait()

        def step(rows):
            mean = (wide(p_buf[1, rows]) + wide(pc_buf[yl, rows]) + wide(py_buf[rows])) / islands
            momentum = decay_rate * m_buf[rows] + mean
            weight = g_buf[rows] - outer_rate * (mean + decay_rate * momentum)
            m_buf[rows] = momentum
            g_buf[rows] = weight
            p_buf[1, rows] = weight.astype(jnp.bfloat16)

        by_tile(step)
        for copy in (fresh_y, fresh_c, fresh_own, ng_out, nm_out):
            copy.start()

    def relay():
        fresh_y.wait()
        relay_c.start()

    lends = [remote(fresh.at[half(i)], lent.at[half(i)], back_send.at[2, i], back_recv.at[2, i], beside((1, 3)[i], 1)) for i in (0, 1)]

    def lend():
        fresh_c.wait()
        fresh_own.wait()
        relay_c.wait()

        @pl.when(role == 1)
        def _():
            for copy in lends:
                copy.start()

    def fresh_load(source, index, slot):
        return pltpu.make_async_copy(quarter(source, index), p_buf.at[slot], load_sem.at[8 + slot])

    def start_fresh(index, slot):
        only(0, fresh_load(fresh, index, slot).start)
        only(1, fresh_load(lent, index, slot).start)

    def blend_all(started):
        @pl.when(role == 1)
        def _():
            for copy in lends:
                copy.wait()

        start_fresh(0, 0)
        for index in range(4):
            slot = index % 2
            fresh_load(fresh, index, slot).wait()
            if index < 3:
                start_fresh(index + 1, 1 - slot)

            def step(rows, slot=slot, index=index):
                for side in (0, 1):
                    first = index * 1024 + side * 512
                    columns = pl.ds(first, 512)
                    base = mix_weight * wide(w_buf[rows, columns]) + (1.0 - mix_weight) * wide(
                        p_buf[slot, rows, pl.ds(side * 512, 512)]
                    )
                    base = base * (1.0 / blend)
                    if first < CUT or started:
                        base = base + acc[rows, columns]
                    acc[rows, columns] = base

            by_tile(step)

    def pair_tokens(pair):
        return pl.ds(pl.multiple_of(mp_at(z + 4 - pair[0], x + 4 - pair[1], 0) * SHARD, 2 * SHARD), 2 * SHARD)

    def hg_out(tokens):
        return pltpu.make_async_copy(part.at[:, tokens], hidden_grad.at[:, tokens], hg_sem.at[0])

    def hg_back(i, tokens):
        return remote(
            part.at[half(i), tokens], hidden_grad.at[half(i), tokens], hg_send.at[i], hg_recv.at[i], beside((3, 1)[i], 1)
        )

    def hg(span, pair, start):
        tokens = pair_tokens(pair)
        if span == 0 and start:
            only(0, w_load.wait)

            @pl.when(role == 1)
            def _():
                for copy in swaps[:2]:
                    copy.wait()

        first, columns = SPANS[span]
        block = lax.dot_general(
            w_buf[:, pl.ds(first, columns)],
            c_bufs[span][tokens],
            (((1,), (1,)), ((), ())),
            preferred_element_type=jnp.float32,
        )
        if span == 0:
            part[:, tokens] = (block * backward_scale).astype(jnp.bfloat16)
            return
        part[:, tokens] = (wide(part[:, tokens]) + block * backward_scale).astype(jnp.bfloat16)

        @pl.when(role == 0)
        def _():
            hg_out(tokens).start()

        @pl.when(role == 1)
        def _():
            for i in (0, 1):
                hg_back(i, tokens).start()

    width = 512

    def product(span, pairs, i):
        columns = pl.ds(pl.multiple_of(i * width, width), width)
        there = pl.ds(pl.multiple_of(SPANS[span][0] + i * width, width), width)
        total = None
        for pair in pairs:
            tokens = pair_tokens(pair)
            block = jnp.dot(h_buf[:, tokens], c_bufs[span][tokens, columns], preferred_element_type=jnp.float32)
            total = block if total is None else total + block
        return there, total

    def wg(span, pairs, start):
        if span == 0 and start:
            only(0, h_load.wait)

            @pl.when(role == 1)
            def _():
                for copy in swaps[2:]:
                    copy.wait()

        def step(i, _):
            there, total = product(span, pairs, i)
            acc[:, there] = total if start else acc[:, there] + total
            return 0

        lax.fori_loop(0, SPANS[span][1] // width, step, 0)

    lo, hi = pl.ds(0, CUT), pl.ds(CUT, D - CUT)
    out_lo = pltpu.make_async_copy(w_buf.at[:, lo], merged.at[:, lo], out_sem.at[2])
    out_hi = pltpu.make_async_copy(w_buf.at[:, hi], merged.at[:, hi], out_sem.at[3])
    back_lo, back_hi = (
        [
            remote(
                w_buf.at[half(i), span], merged.at[half(i), span], back_send.at[j, i], back_recv.at[j, i], beside((3, 1)[i], 1)
            )
            for i in (0, 1)
        ]
        for j, span in enumerate((lo, hi))
    )

    def end0():
        def step(i, _):
            columns = pl.ds(pl.multiple_of(i * width, width), width)
            w_buf[:, columns] = (acc[:, columns] * blend).astype(jnp.bfloat16)
            return 0

        lax.fori_loop(0, CUT // width, step, 0)
        only(0, out_lo.start)

        @pl.when(role == 1)
        def _():
            for copy in back_lo:
                copy.start()

    def end1(pairs):
        def step(i, _):
            there, total = product(1, pairs, i)
            w_buf[:, there] = ((acc[:, there] + total) * blend).astype(jnp.bfloat16)
            return 0

        lax.fori_loop(0, (D - CUT) // width, step, 0)
        only(0, out_hi.start)

        @pl.when(role == 1)
        def _():
            for copy in back_hi:
                copy.start()

    def finish1():
        @pl.when(role == 0)
        def _():
            out_lo.wait()
            out_hi.wait()
            hg_out(pl.ds(0, TOKENS)).wait()

        @pl.when(role == 1)
        def _():
            for copy in back_lo + back_hi:
                copy.wait()
            for i in (0, 1):
                hg_back(i, pl.ds(0, TOKENS)).wait()

    tasks = {
        "swap_w": lambda: swap(0), "swap_h": lambda: swap(1), "reduce": reduce, "outer": outer, "relay": relay, "lend": lend, "blend": blend_all,
        "hg": hg, "wg": wg, "end0": end0, "end1": end1,
    }
    moves = {"seed": seed, "send": send, "wait": wait, "across": across, "other": other}
    steps, sent_rows = plan()[:2]
    for step in steps:
        if step[0] == "task":
            tasks[step[1]](*step[2:])
        else:
            if step[0] == "other" and step[2] == ORIGIN:
                continue
            moves[step[0]](*step[1:])
    finish1()
    ng_out.wait()
    nm_out.wait()
    for span in (0, 1):
        for link in range(len(LINKS)):
            whole = c_bufs[span].at[pl.ds(0, sent_rows[link][span])]
            remote(whole, whole, send_sem.at[link, span], mine_sem.at[0, 0, 0], partner[link]).wait_send()
        whole = c_bufs[span].at[pl.ds(0, 31 * 64)]
        remote(whole, whole, across_sem.at[span], other_sem.at[span, 0], other_core).wait_send()
        only(0, seed_copy(span).wait_send)

        @pl.when(role == 1)
        def _():
            whole = c_bufs[span].at[pl.ds(0, 2 * SHARD)]
            remote(whole, whole, special_sem.at[span], mine_sem.at[0, 0, 0], beside(1, 1)).wait_send()


def body(hidden, cotangent, local_weight, pending, global_weight, outer_momentum):
    big = jax.ShapeDtypeStruct((FF_SHARE, D), jnp.bfloat16)
    state = jax.ShapeDtypeStruct((FF_SHARE, D // islands), jnp.float32)
    dma = pltpu.SemaphoreType.DMA
    outs = pl.pallas_call(
        kernel,
        out_shape=(big, big, state, state, big, big),
        in_specs=[pl.BlockSpec(memory_space=pl.ANY)] * 6,
        out_specs=[pl.BlockSpec(memory_space=pl.ANY)] * 6,
        scratch_shapes=[
            pltpu.VMEM((TOKENS, CUT), jnp.bfloat16),
            pltpu.VMEM((TOKENS, D - CUT), jnp.bfloat16),
            pltpu.VMEM((FF_SHARE, TOKENS), jnp.bfloat16),
            pltpu.VMEM((FF_SHARE, D), jnp.bfloat16),
            pltpu.VMEM((FF_SHARE, D), jnp.float32),
            pltpu.VMEM((FF_SHARE, TOKENS), jnp.bfloat16),
            pltpu.VMEM((2, FF_SHARE, 1024), jnp.bfloat16),
            pltpu.VMEM((2, FF_SHARE, 1024), jnp.bfloat16),
            pltpu.VMEM((FF_SHARE, 1024), jnp.bfloat16),
            pltpu.VMEM((FF_SHARE, 1024), jnp.float32),
            pltpu.VMEM((FF_SHARE, 1024), jnp.float32),
            dma((len(LINKS), 2)),
            dma((2, 2, 32)),
            dma((2,)),
            dma((2, 32)),
            dma((2, 2)),
            dma((2,)),
            dma((2, 2)),
            dma((2, 2)),
            dma((14,)),
            dma((1,)),
            dma((2,)),
            dma((2,)),
            dma((5,)),
            dma((3, 2)),
            dma((3, 2)),
            dma((6,)),
            dma((6,)),
        ],
        compiler_params=pltpu.CompilerParams(collective_id=0, has_side_effects=True, vmem_limit_bytes=63 * MIB),
        cost_estimate=pl.CostEstimate(flops=4 * TOKENS * D * FF_SHARE, bytes_accessed=64 * MIB, transcendentals=0),
        name="gather_and_update",
    )(hidden[0].T, cotangent[0], local_weight[0].T, pending[0].T, global_weight.T, outer_momentum.T)
    return outs[0].T[None], outs[1].T[None], outs[2].T, outs[3].T


def solution(mesh):
    placed = (
        P("island", None, "mp"),
        P("island", "mp", None),
        P("island", None, "mp"),
        P("island", None, "mp"),
        P("island", "mp"),
        P("island", "mp"),
    )
    return jax.shard_map(
        body,
        mesh=mesh,
        in_specs=placed,
        out_specs=(
            P("island", None, "mp"),
            P("island", None, "mp"),
            P("island", "mp"),
            P("island", "mp"),
        ),
        check_vma=False,
    )
```

time: 359 us -> 171 us (0.48)
  waiting for transfers between devices: 288 us -> 0 us
  Pallas kernels: 0 us -> 159 us
  matrix products: 49.5 us -> 0 us
  between operations: 15.5 us -> 0.65 us
  local copies, waits for them, and re-layouts: 0.01 us -> 10.7 us
  other arithmetic: 5.76 us -> 0 us
    all_gather x2 -> x0, waiting for transfers between devices: 171 us -> none  [the longest x1 152 us: body(): piece = lax.all_gather(grads_out, 'mp', axis=0, tiled=True)]
    pallas_call x0 -> x1, Pallas kernels: none -> 159 us  [body(): pl.pallas_call(kernel, out_shape=(big, big, state, state, big, big), in_s...]
    psum x1 -> x0, waiting for transfers between devices: 115 us -> none  [body(): summed_all = lax.psum(pending[0], 'island').astype(jnp.float32)]
    dot_general x2 -> x0, matrix products: 49.5 us -> none  [the longest x1 25.9 us: body(): lax.dot_general(piece, activation, contract_tokens, preferred_element_typ...]
    unnamed x2 -> x10, local copies, waits for them, and re-layouts: 0.01 us -> 10.7 us
    convert_element_type x1 -> x0, other arithmetic: 5.76 us -> none  [body(): new_global.astype(jnp.bfloat16)]
  transfers between devices with their start and end apart: 3 -> 0, of which waited for: 3 -> 0; matrix products, arithmetic and copies ran while one was open for 8% -> 0% of each run, Pallas kernels for 0% -> 0%
where the time goes in v3:
time: 171 us; the launch traced here: 170 us
  Pallas kernels  159 us (93%)
  local copies, waits for them, and re-layouts  10.7 us (6%)
    pallas_call x1, Pallas kernels, body(): pl.pallas_call(kernel, out_shape=(big, big, state, state, big, big), in_s...  159 us
    unnamed x10, local copies, waits for them, and re-layouts  10.7 us

profile of v3, /device:TPU:1, one launch (start us, length us, event | category | flops | bytes accessed | tf_op | source)
XLA Modules:
  0.0 170.2 jit_solution(18047421575264402777)
XLA Ops:
  0.6 158.9 %gather_and_update.1 = (bf16[448,4096]{1,0:T(8,128)(2,1)}, bf16[448,4096]{1,0:T(8,128)(2,1)}, f32[448,1024]{1,0:T(8,128)}, f32[448,1024]{1,0:T(8,128)}, bf16[448...) custom-call(bf16[448,4096]{1,0:T(8,128)(2,1)} %bitcast.24, bf16[128,4096]{1,0:T(8,128)(2,1)} %bitcast.29, ...), custom_call_target="tpu_custom_call" | custom-call | flops 30064771072 | bytes 67108864 | tf_op jit(solution)/shard_map/gather_and_update/pallas_call | solution.py:625
  159.5 0.0 copy-start
  159.5 4.4 %copy.14 = bf16[1,4096,448]{1,2,0:T(8,128)(2,1)} copy(bf16[1,4096,448]{1,2,0:T(8,128)(2,1)} %bitcast.21) | data formatting | bytes 7340032
  164.0 0.0 copy-done
  164.0 0.0 copy-start.2
  164.0 1.9 %copy.15 = bf16[1,4096,448]{1,2,0:T(8,128)(2,1)} copy(bf16[1,4096,448]{1,2,0:T(8,128)(2,1)S(1)} %bitcast.20) | data formatting | bytes 7340032
  165.8 1.0 copy-done.2
  166.8 0.0 copy-start.1
  166.8 1.2 copy.16
  168.0 0.9 copy-done.1
  168.9 1.2 copy.17
Async XLA Ops:
  159.5 4.5 %copy-start = (bf16[448,4096]{1,0:T(8,128)(2,1)S(1)}, bf16[448,4096]{1,0:T(8,128)(2,1)}, u32[]{:S(2)}) copy-start(bf16[448,4096]{1,0:T(8,128)(2,1)} %get-tuple-element.9) | copy-start | bytes 11010052
  164.0 2.8 %copy-start.2 = (f32[448,1024]{1,0:T(8,128)S(1)}, f32[448,1024]{1,0:T(8,128)}, u32[]{:S(2)}) copy-start(f32[448,1024]{1,0:T(8,128)} %get-tuple-element.10) | copy-start | bytes 5505028
  166.8 2.2 %copy-start.1 = (f32[448,1024]{1,0:T(8,128)S(1)}, f32[448,1024]{1,0:T(8,128)}, u32[]{:S(2)}) copy-start(f32[448,1024]{1,0:T(8,128)} %get-tuple-element.11) | copy-start | bytes 5505028

commit v4 on v3

--- a/solution.py
+++ b/solution.py
@@ -536,15 +536,16 @@
     lo, hi = pl.ds(0, CUT), pl.ds(CUT, D - CUT)
     out_lo = pltpu.make_async_copy(w_buf.at[:, lo], merged.at[:, lo], out_sem.at[2])
     out_hi = pltpu.make_async_copy(w_buf.at[:, hi], merged.at[:, hi], out_sem.at[3])
-    back_lo, back_hi = (
-        [
+    def backs(span, j):
+        return [
             remote(
                 w_buf.at[half(i), span], merged.at[half(i), span], back_send.at[j, i], back_recv.at[j, i], beside((3, 1)[i], 1)
             )
             for i in (0, 1)
         ]
-        for j, span in enumerate((lo, hi))
-    )
+
+    back_lo = backs(lo, 0)
+    back_hi = [backs(pl.ds(first, width), 3 + j) for j, first in enumerate(range(CUT, D, width))]
 
     def end0():
         def step(i, _):
@@ -561,18 +562,16 @@
                 copy.start()
 
     def end1(pairs):
-        def step(i, _):
+        for i in range((D - CUT) // width):
             there, total = product(1, pairs, i)
             w_buf[:, there] = ((acc[:, there] + total) * blend).astype(jnp.bfloat16)
-            return 0
-
-        lax.fori_loop(0, (D - CUT) // width, step, 0)
+
+            @pl.when(role == 1)
+            def _(i=i):
+                for copy in back_hi[i]:
+                    copy.start()
+
         only(0, out_hi.start)
-
-        @pl.when(role == 1)
-        def _():
-            for copy in back_hi:
-                copy.start()
 
     def finish1():
         @pl.when(role == 0)
@@ -583,7 +582,7 @@
 
         @pl.when(role == 1)
         def _():
-            for copy in back_lo + back_hi:
+            for copy in sum(back_hi, back_lo):
                 copy.wait()
             for i in (0, 1):
                 hg_back(i, pl.ds(0, TOKENS)).wait()
@@ -616,6 +615,27 @@
         def _():
             whole = c_bufs[span].at[pl.ds(0, 2 * SHARD)]
             remote(whole, whole, special_sem.at[span], mine_sem.at[0, 0, 0], beside(1, 1)).wait_send()
+
+
+def hand_on(*refs):
+    sources, targets, bufs, sems = refs[:4], refs[4:8], refs[8:12], refs[12]
+    ins, outs = [], []
+    for source, target, buf in zip(sources, targets, bufs):
+        rows = source.shape[0] // SPLIT
+        for i in range(SPLIT):
+            part = pl.ds(i * rows, rows)
+            ins.append(pltpu.make_async_copy(source.at[part], buf.at[part], sems.at[len(ins)]))
+            outs.append(pltpu.make_async_copy(buf.at[part], target.at[part], sems.at[len(outs) + 4 * SPLIT]))
+    for copy in ins:
+        copy.start()
+    for copy, out in zip(ins, outs):
+        copy.wait()
+        out.start()
+    for out in outs:
+        out.wait()
+
+
+SPLIT = 4
 
 
 def body(hidden, cotangent, local_weight, pending, global_weight, outer_momentum):
@@ -652,8 +672,8 @@
             dma((2,)),
             dma((2,)),
             dma((5,)),
-            dma((3, 2)),
-            dma((3, 2)),
+            dma((7, 2)),
+            dma((7, 2)),
             dma((6,)),
             dma((6,)),
         ],
@@ -661,6 +681,15 @@
         cost_estimate=pl.CostEstimate(flops=4 * TOKENS * D * FF_SHARE, bytes_accessed=64 * MIB, transcendentals=0),
         name="gather_and_update",
     )(hidden[0].T, cotangent[0], local_weight[0].T, pending[0].T, global_weight.T, outer_momentum.T)
+    outs = pl.pallas_call(
+        hand_on,
+        out_shape=(big, big, state, state),
+        in_specs=[pl.BlockSpec(memory_space=pl.ANY)] * 4,
+        out_specs=[pl.BlockSpec(memory_space=pl.ANY)] * 4,
+        scratch_shapes=[pltpu.VMEM((FF_SHARE, D), jnp.bfloat16)] * 2 + [pltpu.VMEM((FF_SHARE, 1024), jnp.float32)] * 2 + [pltpu.SemaphoreType.DMA((8 * SPLIT,))],
+        compiler_params=pltpu.CompilerParams(vmem_limit_bytes=60 * MIB),
+        name="hand_on",
+    )(*outs[:4])
     return outs[0].T[None], outs[1].T[None], outs[2].T, outs[3].T
 
 

time: 171 us -> 169 us (0.988)
  local copies, waits for them, and re-layouts: 10.7 us -> 0 us
  Pallas kernels: 159 us -> 168 us
    unnamed x10 -> x0, local copies, waits for them, and re-layouts: 10.7 us -> none
    pallas_call x0 -> x1, Pallas kernels: none -> 8.62 us  [body(): pl.pallas_call(hand_on, out_shape=(big, big, state, state), in_specs=[pl....]
where the time goes in v4:
time: 169 us; the launch traced here: 168 us
  Pallas kernels  168 us (99%)
    pallas_call x1, Pallas kernels, body(): pl.pallas_call(kernel, out_shape=(big, big, state, state, big, big), in_s...  159 us
    pallas_call x1, Pallas kernels, body(): pl.pallas_call(hand_on, out_shape=(big, big, state, state), in_specs=[pl....  8.62 us

profile of v4, /device:TPU:1, one launch (start us, length us, event | category | flops | bytes accessed | tf_op | source)
XLA Modules:
  0.0 168.4 jit_solution(14667539339917612713)
XLA Ops:
  0.6 159.0 %gather_and_update.1 = (bf16[448,4096]{1,0:T(8,128)(2,1)}, bf16[448,4096]{1,0:T(8,128)(2,1)}, f32[448,1024]{1,0:T(8,128)}, f32[448,1024]{1,0:T(8,128)}, bf16[448...) custom-call(bf16[448,4096]{1,0:T(8,128)(2,1)} %bitcast.20, bf16[128,4096]{1,0:T(8,128)(2,1)} %bitcast.29, ...), custom_call_target="tpu_custom_call" | custom-call | flops 30064771072 | bytes 67108864 | tf_op jit(solution)/shard_map/gather_and_update/pallas_call | solution.py:645
  159.6 8.6 %hand_on.1 = (bf16[448,4096]{1,0:T(8,128)(2,1)}, bf16[448,4096]{1,0:T(8,128)(2,1)}, f32[448,1024]{1,0:T(8,128)}, f32[448,1024]{1,0:T(8,128)}) custom-call(bf16[448,4096]{1,0:T(8,128)(2,1)} %get-tuple-element.12.refs_0_, bf16[448,4096]{1,0:T(8,128)(2,1)} %get-tuple-element.13.refs_1_, f32[448,1024]{1,0:T(8,128)} %get-tuple-element.14.refs_2_, ...), custom_call_target="tpu_custom_call" | custom-call | tf_op jit(solution)/shard_map/hand_on/pallas_call | solution.py:684

commit v5 on v4

--- a/solution.py
+++ b/solution.py
@@ -67,11 +67,11 @@
 ORDER = ("hg0", "wg0", "hg1", "wg1")
 TASK_TIMES = ((1.0, 0.83), (1.15, 0.83))
 DEPTH = 2
-LATENCY = (4.0, 4.0, 5.0, 6.0)
+LATENCY = (3.0, 3.0, 4.0, 5.0)
 ISLAND_AT = 7.0
 SWAP_AT = (18.0, 36.0)
 WORK_AT = (46.0, 64.0)
-SPECIAL_AT = (18.0, 26.0)
+SPECIAL_AT = (16.0, 23.0)
 
 
 def due_of(span, kind, offset):

time: 169 us -> 169 us (level)
  no operation moved by 1% of the time
where the time goes in v5:
time: 169 us
  Pallas kernels  168 us (99%)
    pallas_call x1, Pallas kernels, body(): pl.pallas_call(kernel, out_shape=(big, big, state, state, big, big), in_s...  159 us
    pallas_call x1, Pallas kernels, body(): pl.pallas_call(hand_on, out_shape=(big, big, state, state), in_specs=[pl....  8.62 us

profile of v5, /device:TPU:1, one launch (start us, length us, event | category | flops | bytes accessed | tf_op | source)
XLA Modules:
  0.0 168.8 jit_solution(5296701126143694033)
XLA Ops:
  0.6 159.4 %gather_and_update.1 = (bf16[448,4096]{1,0:T(8,128)(2,1)}, bf16[448,4096]{1,0:T(8,128)(2,1)}, f32[448,1024]{1,0:T(8,128)}, f32[448,1024]{1,0:T(8,128)}, bf16[448...) custom-call(bf16[448,4096]{1,0:T(8,128)(2,1)} %bitcast.20, bf16[128,4096]{1,0:T(8,128)(2,1)} %bitcast.29, ...), custom_call_target="tpu_custom_call" | custom-call | flops 30064771072 | bytes 67108864 | tf_op jit(solution)/shard_map/gather_and_update/pallas_call | solution.py:645
  160.0 8.6 %hand_on.1 = (bf16[448,4096]{1,0:T(8,128)(2,1)}, bf16[448,4096]{1,0:T(8,128)(2,1)}, f32[448,1024]{1,0:T(8,128)}, f32[448,1024]{1,0:T(8,128)}) custom-call(bf16[448,4096]{1,0:T(8,128)(2,1)} %get-tuple-element.12.refs_0_, bf16[448,4096]{1,0:T(8,128)(2,1)} %get-tuple-element.13.refs_1_, f32[448,1024]{1,0:T(8,128)} %get-tuple-element.14.refs_2_, ...), custom_call_target="tpu_custom_call" | custom-call | tf_op jit(solution)/shard_map/hand_on/pallas_call | solution.py:684
